TPU v7x, 128 devices: a whole 4x4x4 slice. The times are simulated.
128 devices in a mesh: node: 16 (over y, z), local: 8 (over x, core).
Axes of the slice: x: 4, y: 4, z: 4, core: 2. Of those that a mesh axis runs over, the one named last changes fastest.
Arguments:
- tokens: bfloat16 [8192, 3584], P(('node', 'local')), may hold values from -6 to 6
- norm_gain: float32 [3584], replicated, may hold values from 0.1 to 1.9
- w_gate: bfloat16 [128, 3584, 1024], P(('node', 'local')), may hold values from -0.09375 to 0.09375
- w_up: bfloat16 [128, 3584, 1024], P(('node', 'local')), may hold values from -0.09375 to 0.09375
- w_down: bfloat16 [128, 1024, 3584], P(('node', 'local')), may hold values from -0.1875 to 0.1875
- expert_ids: int32 [8192, 8], P(('node', 'local')), may hold values from 0 to 127, as said below
- gate_weights: float32 [8192, 8], P(('node', 'local')), may hold values from 0.1 to 0.5
- capacity: int32 [128], replicated, may hold values from 2 to 4, as said below
Outputs:
- mixed: bfloat16 [8192, 3584], P(('node', 'local'))
Inputs may be any that keep to these rules, and one draw needn't show every extreme that they name: `expert_ids`: each row names 8 distinct experts, all within at most 4 node groups; expert e lies in node group e // 8. In every draw one expert with capacity 4 is named by at least 4 tokens of every micro-batch group. Some expert has capacity exactly 4.
All inputs are finite; a program needn't handle non-finite values.
Results may differ from a plain program's by a relative error of at most 0.0047.
Values may be sent and summed in bfloat16 or wider, within the bound.
A program may use at most 128 MiB of HBM per device.

v0:
```python
import functools

import jax
import jax.numpy as jnp
from jax import lax
from jax.experimental import pallas as pl
from jax.experimental.pallas import tpu as pltpu
from jax.sharding import PartitionSpec as P

MESH = pl.DeviceIdType.MESH
F32, BF16 = jnp.float32, jnp.bfloat16

D = 3584
FF = 1024
HALF = D // 2
W = (640, 640, 512)
OFF = (0, 640, 1280)


def device(x, y, z, c):
    return (y * 4 + z, x * 2 + c)


def expert(x, y, z):
    return (y * 4 + z) * 8 + x * 2


def kernel(
    tok_ref, gain_ref, wg_hbm, wu_hbm, wd_hbm, ids_ref, gates_ref, cap_ref, out_ref,
    wg, wu, wd, normed, tokh, metan, meta, pt, gt, tgx, tgy, tgz,
    stx, sty, stz, rows, hid, retx, rety, retz, cmx, cmy, cmz,
    ptx, pty, ptz, rsx, rsy, rsz, tot, sib,
    wsem, sibs, sibr, s1s, s1r, mts, mtr, dsem, xsem, bsem, rsem, ps, pr,
):
    node, local = lax.axis_index("node"), lax.axis_index("local")
    x, y, z, c = local // 2, node // 4, node % 4, local % 2
    sign = 1 - 2 * c
    tg, st, ret, cm, part, rs = (
        (tgx, tgy, tgz), (stx, sty, stz), (retx, rety, retz), (cmx, cmy, cmz), (ptx, pty, ptz), (rsx, rsy, rsz)
    )

    def remote(src, dst, send, recv, to):
        return pltpu.make_async_remote_copy(
            src_ref=src, dst_ref=dst, send_sem=send, recv_sem=recv, device_id=to, device_id_type=MESH
        )

    def await_bytes(ref, sem):
        pltpu.make_async_copy(ref, ref, sem).wait()

    weights = [
        pltpu.make_async_copy(w_hbm.at[0], w_vmem, wsem.at[i])
        for i, (w_hbm, w_vmem) in enumerate(((wg_hbm, wg), (wu_hbm, wu), (wd_hbm, wd)))
    ]

    barrier = pltpu.get_barrier_semaphore()
    partners = 0
    for dx in range(4):
        for dy in range(4):
            for dz in range(4):
                if dx and dy and dz:
                    continue
                for k in range(2):
                    if dx == dy == dz == 0 and k == 0:
                        continue
                    partners += 1
                    pl.semaphore_signal(
                        barrier, inc=1, device_id_type=MESH,
                        device_id=device((x + dx) % 4, (y + dy) % 4, (z + dz) % 4, (c + k) % 2),
                    )

    resid = tok_ref[...].astype(F32)
    scale = lax.rsqrt(jnp.mean(resid * resid, axis=-1, keepdims=True) + 1e-06)
    normed[...] = (resid * scale * gain_ref[...]).astype(BF16)
    for copy in weights:
        copy.start()

    lane = lax.broadcasted_iota(jnp.int32, (64, 128), 1)
    row = lax.broadcasted_iota(jnp.int32, (64, 128), 0)
    hits = [ids_ref[:, k : k + 1] == lane for k in range(8)]
    named = functools.reduce(jnp.logical_or, hits)
    col64 = lax.broadcasted_iota(jnp.int32, (64, 64), 1)
    row64 = lax.broadcasted_iota(jnp.int32, (64, 64), 0)
    earlier = jnp.logical_and(col64 < row64, col64 // 32 == row64 // 32)
    before = jnp.dot(
        earlier.astype(F32).astype(BF16), named.astype(F32).astype(BF16), preferred_element_type=F32
    )
    group = (row // 32 + c * 2).astype(F32)
    place = jnp.where(before < cap_ref[...].astype(F32), group * 4.0 + before, -1.0)
    info = jnp.zeros((64, 128), F32)
    for k in range(8):
        mine = jnp.sum(jnp.where(hits[k], place, 0.0), axis=1, keepdims=True)
        info = jnp.where(lane == k, ids_ref[:, k : k + 1].astype(F32), info)
        info = jnp.where(lane == 8 + k, mine, info)
        info = jnp.where(lane == 16 + k, gates_ref[:, k : k + 1], info)
    own_rows = pl.ds(pl.multiple_of(c * 64, 64), 64)
    other_rows = pl.ds(pl.multiple_of((1 - c) * 64, 64), 64)
    own_cols = pl.ds(pl.multiple_of(c * HALF, 128), HALF)
    other_cols = pl.ds(pl.multiple_of((1 - c) * HALF, 128), HALF)
    metan[own_rows, :] = info
    tokh[own_rows, :] = normed[:, own_cols]

    pl.semaphore_wait(barrier, partners)

    sibling = device(x, y, z, 1 - c)
    swap = (
        remote(normed.at[:, other_cols], tokh.at[own_rows], sibs.at[0], sibr.at[0], sibling),
        remote(metan.at[own_rows], metan.at[own_rows], sibs.at[1], sibr.at[1], sibling),
    )
    for copy in swap:
        copy.start()
    for copy in swap:
        copy.wait()
    meta[0] = jnp.transpose(metan[...])[0:24, :]

    def along(p, d):
        return (x + d * (p == 0)) % 4, (y + d * (p == 1)) % 4, (z + d * (p == 2)) % 4

    firsts = []
    for d in (1, 3, 2):
        for p in range(3):
            to = device(*along(p, d), c)
            n = 3 * p + d - 1
            firsts.append(remote(meta.at[0], meta.at[1 + n], mts.at[n], mtr.at[n], to))
            firsts.append(
                remote(tokh.at[:, pl.ds(OFF[p], W[p])], tg[p].at[d - 1], s1s.at[n], s1r.at[n], to)
            )
    for copy in firsts:
        copy.start()

    ids128 = lax.broadcasted_iota(jnp.int32, (128, 128), 0).astype(F32)

    def tables(n):
        at = jnp.full((128, 128), -1.0, F32)
        weight = jnp.zeros((128, 128), F32)
        for k in range(8):
            hit = meta[n, k : k + 1, :] == ids128
            at = jnp.where(hit, meta[n, 8 + k : 9 + k, :], at)
            weight = jnp.where(hit, meta[n, 16 + k : 17 + k, :], weight)
        pt[n] = at
        gt[n] = weight

    tables(0)
    for copy in firsts:
        copy.wait_recv()

    def more_tables(n, carry):
        tables(n)
        return carry

    lax.fori_loop(1, 10, more_tables, 0)

    slot = lax.broadcasted_iota(jnp.int32, (16, 128), 0).astype(F32)

    def chips(p, q, i):
        if p == 0:
            return x, (y + i // 4) % 4, (z + i % 4) % 4
        if p == 1:
            return (x + 2 * (i // 4) + q) % 4, y, (z + i % 4) % 4
        return (x + 2 * (i // 4) + q) % 4, (y + i % 4) % 4, z

    def table_of(p, d):
        return jnp.where(d == 0, 0, 3 * p + d)

    def picks(p, q, n, base, weighted):
        blocks = []
        for i in range(8):
            e = expert(*chips(p, q, base + i))
            for k in range(2):
                hit = pt[n, pl.ds(e + k, 1), :] == slot
                value = gt[n, pl.ds(e + k, 1), :] if weighted else 1.0
                blocks.append(jnp.where(hit, value, 0.0))
        return jnp.concatenate(blocks, axis=0)

    def stage(q):
        for p in (1, 2):
            for d in range(4):
                source = tokh[:, OFF[p] : OFF[p] + W[p]] if d == 0 else tg[p][d - 1]
                chosen = picks(p, q, 0 if d == 0 else 3 * p + d, 0, False).astype(BF16)
                block = jnp.dot(chosen, source, preferred_element_type=F32).astype(BF16)
                st[p][d, q] = block.reshape(16, 16, W[p])
        for h in range(2):
            d = 2 * h + q
            source = tokh[:, OFF[0] : OFF[0] + W[0]] if d == 0 else tg[0][d - 1]
            for base in (0, 8):
                chosen = picks(0, q, 0 if d == 0 else d, base, False).astype(BF16)
                block = jnp.dot(chosen, source, preferred_element_type=F32).astype(BF16)
                st[0][q, h, base * 2 : base * 2 + 16] = block.reshape(16, 16, W[0])

    def columns(half, p):
        return pl.ds(pl.multiple_of(half * HALF + OFF[p], 128), W[p])

    def exchange(q, back):
        def one(src, dst, sems, cls, to, here):
            @pl.when(here)
            def _():
                pltpu.make_async_copy(src, dst, sems.at[cls, q] if back else sems.at[q]).start()

            @pl.when(jnp.logical_not(here))
            def _():
                remote(
                    src, dst, (bsem if back else dsem).at[cls, q], sems.at[cls, q] if back else sems.at[q], to
                ).start()

        def step(i, carry):
            h, b, k = i // 8, (sign * ((i // 2) % 4) + 4) % 4, i % 2
            if q == 1:
                h = h * sign + c
            dx = 2 * h + q
            i2 = h * 8 + b * 2 + k
            u, v = (sign * (i // 4) + 4) % 4, (sign * (i % 4) + 4) % 4
            if not back:
                one(sty.at[:, q, i2], rows.at[q, h, :, b, :, columns(c, 1)], xsem, 1,
                    device((x + dx) % 4, y, (z + b) % 4, k), jnp.logical_and(dx + b == 0, k == c))
                one(stz.at[:, q, i2], rows.at[q, h, b, :, :, columns(c, 2)], xsem, 2,
                    device((x + dx) % 4, (y + b) % 4, z, k), jnp.logical_and(dx + b == 0, k == c))
                for m in range(2):
                    one(stx.at[q, :, u * 8 + v * 2 + m], rows.at[q, :, u, v, :, columns(c, 0)], xsem, 0,
                        device(x, (y + u) % 4, (z + v) % 4, m), jnp.logical_and(u + v == 0, m == c))
            else:
                one(rows.at[q, h, :, b, :, columns(k, 1)], rety.at[:, q, h * 8 + b * 2 + c], rsem, 1,
                    device((x - dx + 4) % 4, y, (z - b + 4) % 4, k), jnp.logical_and(dx + b == 0, k == c))
                one(rows.at[q, h, b, :, :, columns(k, 2)], retz.at[:, q, h * 8 + b * 2 + c], rsem, 2,
                    device((x - dx + 4) % 4, (y - b + 4) % 4, z, k), jnp.logical_and(dx + b == 0, k == c))
                for m in range(2):
                    one(rows.at[q, :, u, v, :, columns(m, 0)], retx.at[q, :, u * 8 + v * 2 + c], rsem, 0,
                        device(x, (y - u + 4) % 4, (z - v + 4) % 4, m), jnp.logical_and(u + v == 0, m == c))
            return carry

        lax.fori_loop(0, 16, step, 0)

    for q in range(2):
        stage(q)
        exchange(q, False)

    for p in (1, 2):
        for d in range(4):
            for q in range(2):
                block = picks(p, q, 0 if d == 0 else 3 * p + d, 0, True)
                cm[p][d, :, q * 256 : q * 256 + 256] = jnp.transpose(block).astype(BF16)
    for q in range(2):
        for h in range(2):
            d = 2 * h + q
            for base in (0, 8):
                block = picks(0, q, d, base, True)
                cm[0][d, :, base * 32 : base * 32 + 256] = jnp.transpose(block).astype(BF16)

    for copy in weights:
        copy.wait()
    for q in range(2):
        await_bytes(rows.at[q], xsem.at[q])

        def up(n, carry):
            cols = pl.ds(pl.multiple_of(n * 256, 256), 256)
            batch = rows[q].reshape(512, D)
            gate = jnp.dot(batch, wg[:, cols], preferred_element_type=F32)
            lift = jnp.dot(batch, wu[:, cols], preferred_element_type=F32)
            hid[:, cols] = (gate / (1.0 + jnp.exp(-gate)) * lift).astype(BF16)
            return carry

        lax.fori_loop(0, FF // 256, up, 0)

        def down(n, carry):
            cols = pl.ds(pl.multiple_of(n * 512, 512), 512)
            answer = jnp.dot(hid[...], wd[:, cols], preferred_element_type=F32).astype(BF16)
            rows[q, :, :, :, :, cols] = answer.reshape(2, 4, 4, 16, 512)
            return carry

        lax.fori_loop(0, D // 512, down, 0)
        exchange(q, True)

    lasts = []

    def reduce(p, d, answers):
        total = jnp.dot(cm[p][d], answers, preferred_element_type=F32)
        if d == 0:
            tot[:, OFF[p] : OFF[p] + W[p]] = total
        else:
            part[p][d - 1] = total.astype(BF16)
            n = 3 * p + d - 1
            to = device(*along(p, 4 - d), c)
            copy = remote(part[p].at[d - 1], rs[p].at[d - 1], ps.at[n], pr.at[n], to)
            copy.start()
            lasts.append((p, d, copy))

    for q in range(2):
        await_bytes(retx.at[q], rsem.at[0, q])
        for h in range(2):
            reduce(0, 2 * h + q, retx[q, h].reshape(512, W[0]))
    for p in (1, 2):
        for q in range(2):
            await_bytes(ret[p].at[:, q], rsem.at[p, q])
        for d in range(4):
            reduce(p, d, ret[p][d].reshape(512, W[p]))
    for p, d, copy in lasts:
        copy.wait_recv()
    for p in range(3):
        cols = slice(OFF[p], OFF[p] + W[p])
        tot[:, cols] = tot[:, cols] + (
            rs[p][0].astype(F32) + rs[p][1].astype(F32) + rs[p][2].astype(F32)
        )
    last = remote(tot.at[other_rows], sib, sibs.at[2], sibr.at[2], sibling)
    last.start()
    out_ref[:, own_cols] = (tok_ref[:, own_cols].astype(F32) + tot[own_rows, :]).astype(BF16)
    last.wait_recv()
    out_ref[:, other_cols] = (tok_ref[:, other_cols].astype(F32) + sib[...]).astype(BF16)

    last.wait_send()
    for copy in firsts:
        copy.wait_send()
    for p, d, copy in lasts:
        copy.wait_send()
    for sems, boxes in ((dsem, st), (bsem, ret)):
        for q in range(2):
            await_bytes(boxes[0].at[q, :, pl.ds(0, 31)], sems.at[0, q])
            for p in (1, 2):
                await_bytes(boxes[p].at[:, q, pl.ds(0, 15 + q)], sems.at[p, q])


def shards(tokens, norm_gain, w_gate, w_up, w_down, expert_ids, gate_weights, capacity):
    vmem, dma = pltpu.VMEM, pltpu.SemaphoreType.DMA
    whole = pl.BlockSpec(memory_space=pltpu.VMEM)
    hbm = pl.BlockSpec(memory_space=pl.ANY)
    relay = [vmem((2, 2, 32, 16, W[0]), BF16)] + [vmem((4, 2, 16, 16, w), BF16) for w in W[1:]]
    three = [vmem((3, 128, w), BF16) for w in W]
    return pl.pallas_call(
        kernel,
        out_shape=jax.ShapeDtypeStruct(tokens.shape, BF16),
        in_specs=[whole, whole, hbm, hbm, hbm, whole, whole, whole],
        out_specs=whole,
        scratch_shapes=[
            vmem((D, FF), BF16), vmem((D, FF), BF16), vmem((FF, D), BF16),
            vmem((64, D), BF16), vmem((128, HALF), BF16), vmem((128, 128), F32), vmem((10, 24, 128), F32),
            vmem((10, 128, 128), F32), vmem((10, 128, 128), F32),
            *three,
            *relay,
            vmem((2, 2, 4, 4, 16, D), BF16), vmem((512, FF), BF16),
            *relay,
            *[vmem((4, 128, 512), BF16) for _ in range(3)],
            *three,
            *three,
            vmem((128, HALF), F32), vmem((64, HALF), F32),
            dma((3,)), dma((3,)), dma((3,)), dma((9,)), dma((9,)), dma((9,)), dma((9,)),
            dma((3, 2)), dma((2,)), dma((3, 2)), dma((3, 2)), dma((9,)), dma((9,)),
        ],
        compiler_params=pltpu.CompilerParams(
            collective_id=0, has_side_effects=True, vmem_limit_bytes=64 * 2**20
        ),
        cost_estimate=pl.CostEstimate(flops=23 * 10**9, bytes_accessed=23 * 10**6, transcendentals=10**6),
    )(
        tokens, norm_gain.reshape(1, D), w_gate, w_up, w_down, expert_ids, gate_weights,
        capacity.reshape(1, 128),
    )


def solution(mesh):
    both = ("node", "local")
    in_specs = (
        P(both, None), P(), P(both, None, None), P(both, None, None), P(both, None, None),
        P(both, None), P(both, None), P(),
    )
    return jax.shard_map(shards, mesh=mesh, in_specs=in_specs, out_specs=P(both, None), check_vma=False)
```

profile of v0, /device:TPU:1, one launch (start us, length us, event | category | flops | bytes accessed | tf_op | source)
XLA Modules:
  0.0 162.5 jit_solution(10468191917463352643)
XLA Ops:
  0.0 1.3 reshape.6.gain_ref
  1.3 1.4 copy.9.ids_ref
  2.7 1.4 copy.10.gates_ref
  4.1 156.6 %shard_map.82 = bf16[64,3584]{1,0:T(8,128)(2,1)} custom-call(bf16[64,3584]{1,0:T(8,128)(2,1)} %tok_ref.1, f32[1,3584]{1,0:T(1,128)} %reshape.6.gain_ref, bf16[1,3584,1024]{2,1,0:T(8,128)(2,1)} %wg_hbm.1, bf16[1,3584,1024]{2,1,0:T(8,128)(2,1)} %wu_hbm.1, bf16[1,1024,3584]{2,1,0:T(8,128)(2,1)} %wd_hbm.1, s32[64,8]{1,0:T(8,128)} %copy.9.ids_ref, ...), custom_call_target="tpu_custom_call" | custom-call | flops 23000000512 | bytes 23000000 | tf_op jit(solution)/shard_map/pallas_call | solution.py:325
  160.7 1.8 %copy.12 = bf16[64,3584]{1,0:T(8,128)(2,1)} copy(bf16[64,3584]{1,0:T(8,128)(2,1)} %shard_map.82) | data formatting | bytes 917504
where the time goes:
time: 163 us
  Pallas kernels  157 us (96%)
  local copies, waits for them, and re-layouts  5.89 us (4%)
    pallas_call x1, Pallas kernels, shards(): pl.pallas_call(kernel, out_shape=jax.ShapeDtypeStruct(tokens.shape, BF16)...  157 us
    unnamed x3, local copies, waits for them, and re-layouts  4.57 us

commit v1 on v0

--- a/solution.py
+++ b/solution.py
@@ -27,7 +27,7 @@
 
 def kernel(
     tok_ref, gain_ref, wg_hbm, wu_hbm, wd_hbm, ids_ref, gates_ref, cap_ref, out_ref,
-    wg, wu, wd, normed, tokh, metan, meta, pt, gt, tgx, tgy, tgz,
+    wg, wu, wd, normed, tokh, own_info, sib_info, meta, pt, gt, tgx, tgy, tgz,
     stx, sty, stz, rows, hid, retx, rety, retz, cmx, cmy, cmz,
     ptx, pty, ptz, rsx, rsy, rsz, tot, sib,
     wsem, sibs, sibr, s1s, s1r, mts, mtr, dsem, xsem, bsem, rsem, ps, pr,
@@ -70,33 +70,31 @@
 
     resid = tok_ref[...].astype(F32)
     scale = lax.rsqrt(jnp.mean(resid * resid, axis=-1, keepdims=True) + 1e-06)
-    normed[...] = (resid * scale * gain_ref[...]).astype(BF16)
+    normed[...] = (resid * scale * gain_ref[...].reshape(1, D)).astype(BF16)
     for copy in weights:
         copy.start()
 
-    lane = lax.broadcasted_iota(jnp.int32, (64, 128), 1)
-    row = lax.broadcasted_iota(jnp.int32, (64, 128), 0)
-    hits = [ids_ref[:, k : k + 1] == lane for k in range(8)]
+    twice = lambda a: jnp.concatenate([a, a], axis=1)
+    ids = twice(ids_ref[...])
+    names = lax.broadcasted_iota(jnp.int32, (128, 128), 0)
+    lanes = lax.broadcasted_iota(jnp.int32, (128, 128), 1)
+    hits = [ids[k : k + 1, :] == names for k in range(8)]
     named = functools.reduce(jnp.logical_or, hits)
-    col64 = lax.broadcasted_iota(jnp.int32, (64, 64), 1)
-    row64 = lax.broadcasted_iota(jnp.int32, (64, 64), 0)
-    earlier = jnp.logical_and(col64 < row64, col64 // 32 == row64 // 32)
+    earlier = jnp.logical_and(names < lanes, names // 32 == lanes // 32)
     before = jnp.dot(
-        earlier.astype(F32).astype(BF16), named.astype(F32).astype(BF16), preferred_element_type=F32
-    )
-    group = (row // 32 + c * 2).astype(F32)
-    place = jnp.where(before < cap_ref[...].astype(F32), group * 4.0 + before, -1.0)
-    info = jnp.zeros((64, 128), F32)
+        named.astype(F32).astype(BF16), earlier.astype(F32).astype(BF16), preferred_element_type=F32
+    )
+    group = (lanes // 32 % 2 + c * 2).astype(F32)
+    limit = jnp.transpose(jnp.broadcast_to(cap_ref[...].astype(F32), (128, 128)))
+    place = jnp.where(before < limit, group * 4.0 + before, -1.0)
+    own_info[0:8, :] = ids.astype(F32)
     for k in range(8):
-        mine = jnp.sum(jnp.where(hits[k], place, 0.0), axis=1, keepdims=True)
-        info = jnp.where(lane == k, ids_ref[:, k : k + 1].astype(F32), info)
-        info = jnp.where(lane == 8 + k, mine, info)
-        info = jnp.where(lane == 16 + k, gates_ref[:, k : k + 1], info)
+        own_info[8 + k : 9 + k, :] = jnp.sum(jnp.where(hits[k], place, 0.0), axis=0, keepdims=True)
+    own_info[16:24, :] = twice(gates_ref[...])
     own_rows = pl.ds(pl.multiple_of(c * 64, 64), 64)
     other_rows = pl.ds(pl.multiple_of((1 - c) * 64, 64), 64)
     own_cols = pl.ds(pl.multiple_of(c * HALF, 128), HALF)
     other_cols = pl.ds(pl.multiple_of((1 - c) * HALF, 128), HALF)
-    metan[own_rows, :] = info
     tokh[own_rows, :] = normed[:, own_cols]
 
     pl.semaphore_wait(barrier, partners)
@@ -104,16 +102,20 @@
     sibling = device(x, y, z, 1 - c)
     swap = (
         remote(normed.at[:, other_cols], tokh.at[own_rows], sibs.at[0], sibr.at[0], sibling),
-        remote(metan.at[own_rows], metan.at[own_rows], sibs.at[1], sibr.at[1], sibling),
+        remote(own_info, sib_info, sibs.at[1], sibr.at[1], sibling),
     )
     for copy in swap:
         copy.start()
     for copy in swap:
         copy.wait()
-    meta[0] = jnp.transpose(metan[...])[0:24, :]
+    side = lax.broadcasted_iota(jnp.int32, (24, 128), 1) // 64
+    meta[0] = jnp.where(side == c, own_info[...], sib_info[...])
 
     def along(p, d):
-        return (x + d * (p == 0)) % 4, (y + d * (p == 1)) % 4, (z + d * (p == 2)) % 4
+        if p == 0:
+            return (x + d) % 4, y, z
+        on_z = c if p == 1 else 1 - c
+        return x, (y + d * (1 - on_z)) % 4, (z + d * on_z) % 4
 
     firsts = []
     for d in (1, 3, 2):
@@ -140,26 +142,13 @@
         gt[n] = weight
 
     tables(0)
-    for copy in firsts:
-        copy.wait_recv()
-
-    def more_tables(n, carry):
-        tables(n)
-        return carry
-
-    lax.fori_loop(1, 10, more_tables, 0)
-
     slot = lax.broadcasted_iota(jnp.int32, (16, 128), 0).astype(F32)
 
     def chips(p, q, i):
         if p == 0:
             return x, (y + i // 4) % 4, (z + i % 4) % 4
-        if p == 1:
-            return (x + 2 * (i // 4) + q) % 4, y, (z + i % 4) % 4
-        return (x + 2 * (i // 4) + q) % 4, (y + i % 4) % 4, z
-
-    def table_of(p, d):
-        return jnp.where(d == 0, 0, 3 * p + d)
+        on_z = c if p == 1 else 1 - c
+        return (x + 2 * (i // 4) + q) % 4, (y + i % 4 * on_z) % 4, (z + i % 4 * (1 - on_z)) % 4
 
     def picks(p, q, n, base, weighted):
         blocks = []
@@ -171,66 +160,90 @@
                 blocks.append(jnp.where(hit, value, 0.0))
         return jnp.concatenate(blocks, axis=0)
 
-    def stage(q):
+    def stage(q, shifts):
         for p in (1, 2):
-            for d in range(4):
+            for d in shifts:
                 source = tokh[:, OFF[p] : OFF[p] + W[p]] if d == 0 else tg[p][d - 1]
                 chosen = picks(p, q, 0 if d == 0 else 3 * p + d, 0, False).astype(BF16)
                 block = jnp.dot(chosen, source, preferred_element_type=F32).astype(BF16)
                 st[p][d, q] = block.reshape(16, 16, W[p])
-        for h in range(2):
-            d = 2 * h + q
+        for d in shifts:
+            if d % 2 != q:
+                continue
             source = tokh[:, OFF[0] : OFF[0] + W[0]] if d == 0 else tg[0][d - 1]
             for base in (0, 8):
-                chosen = picks(0, q, 0 if d == 0 else d, base, False).astype(BF16)
+                chosen = picks(0, q, d, base, False).astype(BF16)
                 block = jnp.dot(chosen, source, preferred_element_type=F32).astype(BF16)
-                st[0][q, h, base * 2 : base * 2 + 16] = block.reshape(16, 16, W[0])
+                st[0][q, d // 2, base * 2 : base * 2 + 16] = block.reshape(16, 16, W[0])
 
     def columns(half, p):
         return pl.ds(pl.multiple_of(half * HALF + OFF[p], 128), W[p])
 
-    def exchange(q, back):
-        def one(src, dst, sems, cls, to, here):
+    def exchange(q, back, shifts):
+        first, count = shifts
+        near = pl.ds(first, count)
+        half = [d // 2 for d in range(first, first + count) if d % 2 == q]
+        pair = pl.ds(half[0], len(half)) if half else None
+        sends = bsem if back else dsem
+
+        def one(src, dst, p, to, here):
+            arrived = rsem.at[p, q + (back and q == 1 and first == 0)] if back else xsem.at[q]
+
             @pl.when(here)
             def _():
-                pltpu.make_async_copy(src, dst, sems.at[cls, q] if back else sems.at[q]).start()
+                pltpu.make_async_copy(src, dst, arrived).start()
 
             @pl.when(jnp.logical_not(here))
             def _():
-                remote(
-                    src, dst, (bsem if back else dsem).at[cls, q], sems.at[cls, q] if back else sems.at[q], to
-                ).start()
+                remote(src, dst, sends.at[p, q], arrived, to).start()
 
         def step(i, carry):
             h, b, k = i // 8, (sign * ((i // 2) % 4) + 4) % 4, i % 2
             if q == 1:
                 h = h * sign + c
             dx = 2 * h + q
-            i2 = h * 8 + b * 2 + k
             u, v = (sign * (i // 4) + 4) % 4, (sign * (i % 4) + 4) % 4
-            if not back:
-                one(sty.at[:, q, i2], rows.at[q, h, :, b, :, columns(c, 1)], xsem, 1,
-                    device((x + dx) % 4, y, (z + b) % 4, k), jnp.logical_and(dx + b == 0, k == c))
-                one(stz.at[:, q, i2], rows.at[q, h, b, :, :, columns(c, 2)], xsem, 2,
-                    device((x + dx) % 4, (y + b) % 4, z, k), jnp.logical_and(dx + b == 0, k == c))
+            turn = -1 if back else 1
+            here = jnp.logical_and(dx + b == 0, k == c)
+            relay, box = (k, h * 8 + b * 2 + c) if back else (c, h * 8 + b * 2 + k)
+
+            def move(box_ref, rows_ref, p, to, here):
+                one(*((rows_ref, box_ref) if back else (box_ref, rows_ref)), p, to, here)
+
+            if pair is not None:
                 for m in range(2):
-                    one(stx.at[q, :, u * 8 + v * 2 + m], rows.at[q, :, u, v, :, columns(c, 0)], xsem, 0,
-                        device(x, (y + u) % 4, (z + v) % 4, m), jnp.logical_and(u + v == 0, m == c))
-            else:
-                one(rows.at[q, h, :, b, :, columns(k, 1)], rety.at[:, q, h * 8 + b * 2 + c], rsem, 1,
-                    device((x - dx + 4) % 4, y, (z - b + 4) % 4, k), jnp.logical_and(dx + b == 0, k == c))
-                one(rows.at[q, h, b, :, :, columns(k, 2)], retz.at[:, q, h * 8 + b * 2 + c], rsem, 2,
-                    device((x - dx + 4) % 4, (y - b + 4) % 4, z, k), jnp.logical_and(dx + b == 0, k == c))
-                for m in range(2):
-                    one(rows.at[q, :, u, v, :, columns(m, 0)], retx.at[q, :, u * 8 + v * 2 + c], rsem, 0,
-                        device(x, (y - u + 4) % 4, (z - v + 4) % 4, m), jnp.logical_and(u + v == 0, m == c))
+                    relay0, box0 = (m, u * 8 + v * 2 + c) if back else (c, u * 8 + v * 2 + m)
+                    move((retx if back else stx).at[q, pair, box0], rows.at[q, pair, u, v, :, columns(relay0, 0)],
+                         0, device(x, (y + turn * u + 4) % 4, (z + turn * v + 4) % 4, m),
+                         jnp.logical_and(u + v == 0, m == c))
+            for r in range(2):
+                @pl.when((k if back else c) == r)
+                def _():
+                    along_y, along_z = 1 + r, 2 - r
+                    move((ret if back else st)[along_y].at[near, q, box],
+                         rows.at[q, h, near, b, :, columns(relay, along_y)], along_y,
+                         device((x + turn * dx + 4) % 4, y, (z + turn * b + 4) % 4, k), here)
+                    move((ret if back else st)[along_z].at[near, q, box],
+                         rows.at[q, h, b, near, :, columns(relay, along_z)], along_z,
+                         device((x + turn * dx + 4) % 4, (y + turn * b + 4) % 4, z, k), here)
             return carry
 
         lax.fori_loop(0, 16, step, 0)
 
-    for q in range(2):
-        stage(q)
-        exchange(q, False)
+    stage(0, (0,))
+    exchange(0, False, (0, 1))
+    for copy in firsts:
+        copy.wait_recv()
+
+    def more_tables(n, carry):
+        tables(n)
+        return carry
+
+    lax.fori_loop(1, 10, more_tables, 0)
+    stage(0, (1, 2, 3))
+    exchange(0, False, (1, 3))
+    stage(1, (0, 1, 2, 3))
+    exchange(1, False, (0, 4))
 
     for p in (1, 2):
         for d in range(4):
@@ -266,7 +279,11 @@
             return carry
 
         lax.fori_loop(0, D // 512, down, 0)
-        exchange(q, True)
+        if q == 0:
+            exchange(0, True, (0, 4))
+        else:
+            exchange(1, True, (1, 3))
+            exchange(1, True, (0, 1))
 
     lasts = []
 
@@ -287,10 +304,13 @@
         for h in range(2):
             reduce(0, 2 * h + q, retx[q, h].reshape(512, W[0]))
     for p in (1, 2):
-        for q in range(2):
-            await_bytes(ret[p].at[:, q], rsem.at[p, q])
-        for d in range(4):
+        await_bytes(ret[p].at[:, 0], rsem.at[p, 0])
+        await_bytes(ret[p].at[pl.ds(1, 3), 1], rsem.at[p, 1])
+        for d in range(1, 4):
             reduce(p, d, ret[p][d].reshape(512, W[p]))
+    for p in (1, 2):
+        await_bytes(ret[p].at[0, 1], rsem.at[p, 2])
+        reduce(p, 0, ret[p][0].reshape(512, W[p]))
     for p, d, copy in lasts:
         copy.wait_recv()
     for p in range(3):
@@ -329,7 +349,7 @@
         out_specs=whole,
         scratch_shapes=[
             vmem((D, FF), BF16), vmem((D, FF), BF16), vmem((FF, D), BF16),
-            vmem((64, D), BF16), vmem((128, HALF), BF16), vmem((128, 128), F32), vmem((10, 24, 128), F32),
+            vmem((64, D), BF16), vmem((128, HALF), BF16), vmem((24, 128), F32), vmem((24, 128), F32), vmem((10, 24, 128), F32),
             vmem((10, 128, 128), F32), vmem((10, 128, 128), F32),
             *three,
             *relay,
@@ -340,14 +360,14 @@
             *three,
             vmem((128, HALF), F32), vmem((64, HALF), F32),
             dma((3,)), dma((3,)), dma((3,)), dma((9,)), dma((9,)), dma((9,)), dma((9,)),
-            dma((3, 2)), dma((2,)), dma((3, 2)), dma((3, 2)), dma((9,)), dma((9,)),
+            dma((3, 2)), dma((2,)), dma((3, 2)), dma((3, 3)), dma((9,)), dma((9,)),
         ],
         compiler_params=pltpu.CompilerParams(
             collective_id=0, has_side_effects=True, vmem_limit_bytes=64 * 2**20
         ),
         cost_estimate=pl.CostEstimate(flops=23 * 10**9, bytes_accessed=23 * 10**6, transcendentals=10**6),
     )(
-        tokens, norm_gain.reshape(1, D), w_gate, w_up, w_down, expert_ids, gate_weights,
+        tokens, norm_gain, w_gate, w_up, w_down, expert_ids.T, gate_weights.T,
         capacity.reshape(1, 128),
     )
 

time: 163 us -> 148 us (0.908); the launches traced: 163 us -> 146 us
  Pallas kernels: 157 us -> 144 us
  local copies, waits for them, and re-layouts: 5.89 us -> 1.82 us
    pallas_call x1, Pallas kernels: 157 us -> 144 us  [shards(): pl.pallas_call(kernel, out_shape=jax.ShapeDtypeStruct(tokens.shape, BF16)...]
    unnamed x3 -> x1, local copies, waits for them, and re-layouts: 4.57 us -> 1.82 us
where the time goes in v1:
time: 148 us; the launch traced here: 146 us
  Pallas kernels  144 us (97%)
  local copies, waits for them, and re-layouts  1.82 us (1%)
    pallas_call x1, Pallas kernels, shards(): pl.pallas_call(kernel, out_shape=jax.ShapeDtypeStruct(tokens.shape, BF16)...  144 us

profile of v1, /device:TPU:1, one launch (start us, length us, event | category | flops | bytes accessed | tf_op | source)
XLA Modules:
  0.0 145.8 jit_solution(6909530501993859811)
XLA Ops:
  0.0 143.9 %shard_map.82 = bf16[64,3584]{1,0:T(8,128)(2,1)} custom-call(bf16[64,3584]{1,0:T(8,128)(2,1)} %tok_ref.1, f32[3584]{0:T(1024)} %gain_ref.1, bf16[1,3584,1024]{2,1,0:T(8,128)(2,1)} %wg_hbm.1, bf16[1,3584,1024]{2,1,0:T(8,128)(2,1)} %wu_hbm.1, bf16[1,1024,3584]{2,1,0:T(8,128)(2,1)} %wd_hbm.1, s32[8,64]{1,0:T(8,128)} %bitcast.3, f32[8,64]{1,0:T(8,128)} %bitcast.4, ...), custom_call_target="tpu_custom_call" | custom-call | flops 23000000512 | bytes 23000000 | tf_op jit(solution)/shard_map/pallas_call | solution.py:345
  144.0 1.8 %copy.10 = bf16[64,3584]{1,0:T(8,128)(2,1)} copy(bf16[64,3584]{1,0:T(8,128)(2,1)} %shard_map.82) | data formatting | bytes 917504

commit v2 on v1

v2 whole, which is shorter than its diff:
```python
import functools

import jax
import jax.numpy as jnp
from jax import lax
from jax.experimental import pallas as pl
from jax.experimental.pallas import tpu as pltpu
from jax.sharding import PartitionSpec as P

MESH = pl.DeviceIdType.MESH
F32, BF16 = jnp.float32, jnp.bfloat16

D = 3584
FF = 1024
HALF = D // 2
W = (640, 640, 512)
OFF = (0, 640, 1280)
AXES = ((0, 1, 2), (1, 2, 0), (2, 0, 1))
NOW = 4
PLACE = (0, 2, 1, 3)
KINDS = ((0, 0, 0), (1, 2, 8), (2, 3, 16), (1, 1, 24), (2, 1, 28))


def device(x, y, z, c):
    return (y * 4 + z, x * 2 + c)


def expert(x, y, z):
    return (y * 4 + z) * 8 + x * 2


def kernel(
    tok_ref, gain_ref, wg_hbm, wu_hbm, wd_hbm, ids_ref, gates_ref, cap_ref, out_ref,
    wg, wu, wd, normed, tokh, own_info, sib_info, meta, tk0, tk1, tk2,
    st0, st1, st2, rows, hid, ret0, ret1, ret2, line, far,
    rb0, rb1, rb2, rs0, rs1, rs2, tot, sib,
    wsem, sibs, sibr, s1s, s1r, mts, mtr, s2s, s2r, m2s, m2r, dsem, xsem, bsem, rsem, qs, qr, ps, pr,
):
    node, local = lax.axis_index("node"), lax.axis_index("local")
    x, y, z, c = local // 2, node // 4, node % 4, local % 2
    sign = 1 - 2 * c
    tk, st, ret, rb, rs = (tk0, tk1, tk2), (st0, st1, st2), (ret0, ret1, ret2), (rb0, rb1, rb2), (rs0, rs1, rs2)

    def chip(p, da, db, dc):
        place = [x, y, z]
        for axis, d in zip(AXES[p], (da, db, dc)):
            place[axis] = (place[axis] + d + 4) % 4
        return place

    def remote(src, dst, send, recv, to):
        return pltpu.make_async_remote_copy(
            src_ref=src, dst_ref=dst, send_sem=send, recv_sem=recv, device_id=to, device_id_type=MESH
        )

    def await_bytes(ref, sem):
        pltpu.make_async_copy(ref, ref, sem).wait()

    weights = [
        pltpu.make_async_copy(w_hbm.at[0], w_vmem, wsem.at[i])
        for i, (w_hbm, w_vmem) in enumerate(((wg_hbm, wg), (wu_hbm, wu), (wd_hbm, wd)))
    ]

    barrier = pltpu.get_barrier_semaphore()
    partners = 0
    for dx in range(4):
        for dy in range(4):
            for dz in range(4):
                if dx and dy and dz:
                    continue
                for k in range(2):
                    if dx == dy == dz == 0 and k == 0:
                        continue
                    partners += 1
                    pl.semaphore_signal(
                        barrier, inc=1, device_id_type=MESH,
                        device_id=device((x + dx) % 4, (y + dy) % 4, (z + dz) % 4, (c + k) % 2),
                    )

    resid = tok_ref[...].astype(F32)
    scale = lax.rsqrt(jnp.mean(resid * resid, axis=-1, keepdims=True) + 1e-06)
    normed[...] = (resid * scale * gain_ref[...].reshape(1, D)).astype(BF16)
    for copy in weights:
        copy.start()

    twice = lambda a: jnp.concatenate([a, a], axis=1)
    ids = twice(ids_ref[...])
    names = lax.broadcasted_iota(jnp.int32, (128, 128), 0)
    lanes = lax.broadcasted_iota(jnp.int32, (128, 128), 1)
    hits = [ids[k : k + 1, :] == names for k in range(8)]
    named = functools.reduce(jnp.logical_or, hits)
    earlier = jnp.logical_and(names < lanes, names // 32 == lanes // 32)
    before = jnp.dot(
        named.astype(F32).astype(BF16), earlier.astype(F32).astype(BF16), preferred_element_type=F32
    )
    group = (lanes // 32 % 2 + c * 2).astype(F32)
    limit = jnp.transpose(jnp.broadcast_to(cap_ref[...].astype(F32), (128, 128)))
    place = jnp.where(before < limit, group * 4.0 + before, -1.0)
    own_info[0:8, :] = ids.astype(F32)
    for k in range(8):
        own_info[8 + k : 9 + k, :] = jnp.sum(jnp.where(hits[k], place, 0.0), axis=0, keepdims=True)
    own_info[16:24, :] = twice(gates_ref[...])
    own_rows = pl.ds(pl.multiple_of(c * 64, 64), 64)
    other_rows = pl.ds(pl.multiple_of((1 - c) * 64, 64), 64)
    own_cols = pl.ds(pl.multiple_of(c * HALF, 128), HALF)
    other_cols = pl.ds(pl.multiple_of((1 - c) * HALF, 128), HALF)
    tokh[own_rows, :] = normed[:, own_cols]

    pl.semaphore_wait(barrier, partners)

    sibling = device(x, y, z, 1 - c)
    swap = (
        remote(normed.at[:, other_cols], tokh.at[own_rows], sibs.at[0], sibr.at[0], sibling),
        remote(own_info, sib_info, sibs.at[1], sibr.at[1], sibling),
    )
    for copy in swap:
        copy.start()
    for copy in swap:
        copy.wait()
    side = lax.broadcasted_iota(jnp.int32, (24, 128), 1) // 64
    for p in range(3):
        meta[p, 0, 0] = jnp.where(side == c, own_info[...], sib_info[...])
        tk[p][0, 0] = tokh[:, OFF[p] : OFF[p] + W[p]]

    firsts, seconds, thirds = [], [], []
    for d in (1, 3, 2):
        for p in range(3):
            to = device(*chip(p, d, 0, 0), c)
            n = 3 * p + d - 1
            firsts.append(remote(meta.at[p, 0, 0], meta.at[p, 0, PLACE[d]], mts.at[n], mtr.at[n], to))
            firsts.append(remote(tk[p].at[0, 0], tk[p].at[0, PLACE[d]], s1s.at[n], s1r.at[n], to))
    for copies, m, span in ((seconds, 0, pl.ds(0, 1)), (thirds, 1, pl.ds(1, 3))):
        for b in (1, 2):
            for p in range(3):
                to = device(*chip(p, 0, 3 - 2 * b, 0), c)
                n = 4 * p + 2 * (b - 1) + m
                copies.append(remote(meta.at[p, 0, span], meta.at[p, b, span], m2s.at[n], m2r.at[n], to))
                copies.append(remote(tk[p].at[0, span], tk[p].at[b, span], s2s.at[n], s2r.at[n], to))
    for copy in firsts + seconds:
        copy.start()

    slot = lax.broadcasted_iota(jnp.int32, (16, 128), 0).astype(F32)

    def stage(p, b):
        behind = 3 - 2 * b
        groups = [[(chip(p, 0, 0, g), k) for g in range(4) for k in range(2)]]
        if b:
            groups.append([(chip(p, 0, behind, g), b - 1) for g in range(4)])

        def step(a, carry):
            ids, place, gate = meta[p, b, a, 0:8, :], meta[p, b, a, 8:16, :], meta[p, b, a, 16:24, :]
            source = tk[p][b, a]
            for far_off, group in enumerate(groups):
                picks, weights = [], []
                for where, k in group:
                    mine = ids == (expert(*where) + k).astype(F32)
                    at = jnp.sum(jnp.where(mine, place + 1.0, 0.0), axis=0, keepdims=True) - 1.0
                    weight = jnp.sum(jnp.where(mine, gate, 0.0), axis=0, keepdims=True)
                    hit = at == slot
                    picks.append(jnp.where(hit, 1.0, 0.0))
                    weights.append(jnp.where(hit, weight, 0.0))
                chosen = jnp.concatenate(picks, axis=0).astype(BF16)
                weighted = jnp.concatenate(weights, axis=0).astype(BF16)
                block = jnp.dot(chosen, source, preferred_element_type=F32).astype(BF16)
                if far_off:
                    far[p, b - 1, a] = weighted
                    st[p][20 + 4 * b : 24 + 4 * b, a] = block.reshape(4, 16, W[p])
                else:
                    line[p, b, a] = weighted
                    st[p][8 * b : 8 * b + 8, a] = block.reshape(8, 16, W[p])
            return carry

        lax.fori_loop(0, 4, step, 0)

    def columns(half, p):
        return pl.ds(pl.multiple_of(half * HALF + OFF[p], 128), W[p])

    def exchange(q, back, kinds):
        dx = PLACE[q]
        sends = bsem if back else dsem

        def message(p, kind, g, k):
            b, place_b, base = KINDS[kind]
            distant = kind > 2
            behind = (3 - 2 * b) if distant else 0
            place_c = q if p == 1 else g % 2 * 2 + g // 2
            span = q if p == 0 else pl.ds(0, 4)
            cols = columns(k if back else c, p)
            if p == 0:
                there = rows.at[span, place_b, place_c, :, cols]
            elif p == 1:
                there = rows.at[place_c, span, place_b, :, cols]
            else:
                there = rows.at[place_b, place_c, span, :, cols]
            box = ret[p] if back else st[p]
            number = base + g if distant else base + g * 2 + (c if back else k)
            box = box.at[number, span]
            turn = -1 if back else 1
            to = device(*chip(p, 0, turn * behind, turn * g), k)
            src, dst = (there, box) if back else (box, there)
            arrived = rsem.at[p, int(kind == 0)] if back else xsem.at[q]
            if distant:
                remote(src, dst, sends.at[p], arrived, to).start()
                return
            here = jnp.logical_and(g == 0, k == c)

            @pl.when(here)
            def _():
                pltpu.make_async_copy(src, dst, arrived).start()

            @pl.when(jnp.logical_not(here))
            def _():
                remote(src, dst, sends.at[p], arrived, to).start()

        def step(i, carry):
            g = (sign * i + 4) % 4

            def lines(kind, ks):
                for p in (0, 2):
                    if p == 0 or KINDS[kind][1] == q:
                        for k in ks:
                            message(p, kind, g, k)

            for kind in kinds:
                only = KINDS[kind][0] - 1
                if kind < 3:
                    lines(kind, (0, 1))

                    @pl.when(i % 2 == 0)
                    def _():
                        message(1, kind, dx, i // 2)
                elif back:
                    @pl.when(c == only)
                    def _():
                        lines(kind, (0, 1))

                        @pl.when(i % 2 == 0)
                        def _():
                            message(1, kind, dx, i // 2)
                else:
                    lines(kind, (only,))

                    @pl.when(i == 0)
                    def _():
                        message(1, kind, dx, only)
            return carry

        lax.fori_loop(0, 4, step, 0)

    for copy in firsts:
        copy.wait_recv()
    for copy in thirds:
        copy.start()
    for p in range(3):
        stage(p, 0)
    for q in range(4):
        exchange(q, False, (0,))
    for copy in seconds + thirds:
        copy.wait_recv()
    for b in (1, 2):
        for p in range(3):
            stage(p, b)
    for q in range(4):
        exchange(q, False, (1, 2, 3, 4))

    for copy in weights:
        copy.wait()
    for q in range(4):
        await_bytes(rows.at[q], xsem.at[q])

        def up(n, carry):
            cols = pl.ds(pl.multiple_of(n * 256, 256), 256)
            batch = rows[q].reshape(256, D)
            gate = jnp.dot(batch, wg[:, cols], preferred_element_type=F32)
            lift = jnp.dot(batch, wu[:, cols], preferred_element_type=F32)
            hid[:, cols] = (gate / (1.0 + jnp.exp(-gate)) * lift).astype(BF16)
            return carry

        lax.fori_loop(0, FF // 256, up, 0)

        def down(n, carry):
            cols = pl.ds(pl.multiple_of(n * 512, 512), 512)
            answer = jnp.dot(hid[...], wd[:, cols], preferred_element_type=F32).astype(BF16)
            rows[q, :, :, :, cols] = answer.reshape(4, 4, 16, 512)
            return carry

        lax.fori_loop(0, D // 512, down, 0)
        exchange(q, True, (1, 2, 3, 4) if q >= NOW else (0, 1, 2, 3, 4))
    for q in range(NOW, 4):
        exchange(q, True, (0,))

    for copy in firsts + seconds + thirds:
        copy.wait_send()

    def weigh(weighted, answers):
        return lax.dot_general(weighted, answers, (((0,), (0,)), ((), ())), preferred_element_type=F32)

    homeward = []
    for p in range(3):
        await_bytes(ret[p].at[pl.ds(8, 24)], rsem.at[p, 0])
        for b in (1, 2):
            def step(a, carry):
                near = weigh(line[p, b, a], ret[p][8 * b : 8 * b + 8, a].reshape(128, W[p]))
                away = weigh(far[p, b - 1, a], ret[p][20 + 4 * b : 24 + 4 * b, a].reshape(64, W[p]))
                tk[p][b, a] = (near + away).astype(BF16)
                return carry

            lax.fori_loop(0, 4, step, 0)
            n = 2 * p + b - 1
            to = device(*chip(p, 0, 2 * b - 3, 0), c)
            copy = remote(tk[p].at[b], rb[p].at[b - 1], qs.at[n], qr.at[n], to)
            copy.start()
            homeward.append(copy)
    lasts = []
    for p in range(3):
        await_bytes(ret[p].at[pl.ds(0, 8)], rsem.at[p, 1])
        for copy in homeward[2 * p : 2 * p + 2]:
            copy.wait_recv()
        for d in (2, 1, 3, 0):
            a = PLACE[d]
            total = weigh(line[p, 0, a], ret[p][0:8, a].reshape(128, W[p]))
            total = total + (rb[p][0, a].astype(F32) + rb[p][1, a].astype(F32))
            if d == 0:
                tot[:, OFF[p] : OFF[p] + W[p]] = total
            else:
                tk[p][0, a] = total.astype(BF16)
                n = 3 * p + d - 1
                to = device(*chip(p, -d, 0, 0), c)
                copy = remote(tk[p].at[0, a], rs[p].at[a - 1], ps.at[n], pr.at[n], to)
                copy.start()
                lasts.append(copy)
    for copy in lasts:
        copy.wait_recv()
    for p in range(3):
        cols = slice(OFF[p], OFF[p] + W[p])
        tot[:, cols] = tot[:, cols] + (
            rs[p][0].astype(F32) + rs[p][1].astype(F32) + rs[p][2].astype(F32)
        )
    last = remote(tot.at[other_rows], sib, sibs.at[2], sibr.at[2], sibling)
    last.start()
    out_ref[:, own_cols] = (tok_ref[:, own_cols].astype(F32) + tot[own_rows, :]).astype(BF16)
    last.wait_recv()
    out_ref[:, other_cols] = (tok_ref[:, other_cols].astype(F32) + sib[...]).astype(BF16)

    last.wait_send()
    for copy in homeward + lasts:
        copy.wait_send()
    for sems, boxes in ((dsem, st), (bsem, ret)):
        for p in range(3):
            await_bytes(boxes[p].at[pl.ds(0, 29)], sems.at[p])


def shards(tokens, norm_gain, w_gate, w_up, w_down, expert_ids, gate_weights, capacity):
    vmem, dma = pltpu.VMEM, pltpu.SemaphoreType.DMA
    whole = pl.BlockSpec(memory_space=pltpu.VMEM)
    hbm = pl.BlockSpec(memory_space=pl.ANY)
    relay = [vmem((32, 4, 16, w), BF16) for w in W]
    return pl.pallas_call(
        kernel,
        out_shape=jax.ShapeDtypeStruct(tokens.shape, BF16),
        in_specs=[whole, whole, hbm, hbm, hbm, whole, whole, whole],
        out_specs=whole,
        scratch_shapes=[
            vmem((D, FF), BF16), vmem((D, FF), BF16), vmem((FF, D), BF16),
            vmem((64, D), BF16), vmem((128, HALF), BF16),
            vmem((24, 128), F32), vmem((24, 128), F32), vmem((3, 3, 4, 24, 128), F32),
            *[vmem((3, 4, 128, w), BF16) for w in W],
            *relay,
            vmem((4, 4, 4, 16, D), BF16), vmem((256, FF), BF16),
            *relay,
            vmem((3, 3, 4, 128, 128), BF16), vmem((3, 2, 4, 64, 128), BF16),
            *[vmem((2, 4, 128, w), BF16) for w in W],
            *[vmem((3, 128, w), BF16) for w in W],
            vmem((128, HALF), F32), vmem((64, HALF), F32),
            dma((3,)), dma((3,)), dma((3,)), dma((9,)), dma((9,)), dma((9,)), dma((9,)),
            dma((12,)), dma((12,)), dma((12,)), dma((12,)),
            dma((3,)), dma((4,)), dma((3,)), dma((3, 2)), dma((6,)), dma((6,)), dma((9,)), dma((9,)),
        ],
        compiler_params=pltpu.CompilerParams(
            collective_id=0, has_side_effects=True, vmem_limit_bytes=64 * 2**20
        ),
        cost_estimate=pl.CostEstimate(flops=23 * 10**9, bytes_accessed=23 * 10**6, transcendentals=10**6),
    )(
        tokens, norm_gain, w_gate, w_up, w_down, expert_ids.T, gate_weights.T,
        capacity.reshape(1, 128),
    )


def solution(mesh):
    both = ("node", "local")
    in_specs = (
        P(both, None), P(), P(both, None, None), P(both, None, None), P(both, None, None),
        P(both, None), P(both, None), P(),
    )
    return jax.shard_map(shards, mesh=mesh, in_specs=in_specs, out_specs=P(both, None), check_vma=False)
```

time: 148 us -> 143 us (0.966); the launches traced: 146 us -> 143 us
  Pallas kernels: 144 us -> 141 us
    pallas_call x1, Pallas kernels: 144 us -> 141 us  [shards(): pl.pallas_call(kernel, out_shape=jax.ShapeDtypeStruct(tokens.shape, BF16)...]
where the time goes in v2:
time: 143 us
  Pallas kernels  141 us (99%)
  local copies, waits for them, and re-layouts  1.82 us (1%)
    pallas_call x1, Pallas kernels, shards(): pl.pallas_call(kernel, out_shape=jax.ShapeDtypeStruct(tokens.shape, BF16)...  141 us

profile of v2, /device:TPU:1, one launch (start us, length us, event | category | flops | bytes accessed | tf_op | source)
XLA Modules:
  0.0 143.2 jit_solution(13762118304116889114)
XLA Ops:
  0.0 141.4 %shard_map.82 = bf16[64,3584]{1,0:T(8,128)(2,1)} custom-call(bf16[64,3584]{1,0:T(8,128)(2,1)} %tok_ref.1, f32[3584]{0:T(1024)} %gain_ref.1, bf16[1,3584,1024]{2,1,0:T(8,128)(2,1)} %wg_hbm.1, bf16[1,3584,1024]{2,1,0:T(8,128)(2,1)} %wu_hbm.1, bf16[1,1024,3584]{2,1,0:T(8,128)(2,1)} %wd_hbm.1, s32[8,64]{1,0:T(8,128)} %bitcast.3, f32[8,64]{1,0:T(8,128)} %bitcast.4, ...), custom_call_target="tpu_custom_call" | custom-call | flops 23000000512 | bytes 23000000 | tf_op jit(solution)/shard_map/pallas_call | solution.py:357
  141.4 1.8 %copy.10 = bf16[64,3584]{1,0:T(8,128)(2,1)} copy(bf16[64,3584]{1,0:T(8,128)(2,1)} %shard_map.82) | data formatting | bytes 917504

commit v3 on v2

--- a/solution.py
+++ b/solution.py
@@ -41,11 +41,16 @@
     sign = 1 - 2 * c
     tk, st, ret, rb, rs = (tk0, tk1, tk2), (st0, st1, st2), (ret0, ret1, ret2), (rb0, rb1, rb2), (rs0, rs1, rs2)
 
-    def chip(p, da, db, dc):
+    def moved(t, da, db, dc):
         place = [x, y, z]
-        for axis, d in zip(AXES[p], (da, db, dc)):
+        for axis, d in zip(AXES[t], (da, db, dc)):
             place[axis] = (place[axis] + d + 4) % 4
         return place
+
+    def chip(p, da, db, dc):
+        if p == 0:
+            return moved(0, da, db, dc)
+        return [jnp.where(c == 0, u, v) for u, v in zip(moved(p, da, db, dc), moved(3 - p, da, db, dc))]
 
     def remote(src, dst, send, recv, to):
         return pltpu.make_async_remote_copy(
@@ -65,7 +70,7 @@
     for dx in range(4):
         for dy in range(4):
             for dz in range(4):
-                if dx and dy and dz:
+                if dx and dy and dz or (dx, dy) == (0, 2) and dz or (dy, dz) == (0, 2) and dx or (dz, dx) == (0, 2) and dy:
                     continue
                 for k in range(2):
                     if dx == dy == dz == 0 and k == 0:
@@ -165,7 +170,7 @@
                     far[p, b - 1, a] = weighted
                     st[p][20 + 4 * b : 24 + 4 * b, a] = block.reshape(4, 16, W[p])
                 else:
-                    line[p, b, a] = weighted
+                    line[p, b, a] = jnp.transpose(jnp.concatenate(weights, axis=0)).astype(BF16)
                     st[p][8 * b : 8 * b + 8, a] = block.reshape(8, 16, W[p])
             return carry
 
@@ -178,16 +183,17 @@
         dx = PLACE[q]
         sends = bsem if back else dsem
 
-        def message(p, kind, g, k):
+        def message(t, r, kind, g, k):
+            p = 3 - t if t and r else t
             b, place_b, base = KINDS[kind]
             distant = kind > 2
             behind = (3 - 2 * b) if distant else 0
-            place_c = q if p == 1 else g % 2 * 2 + g // 2
-            span = q if p == 0 else pl.ds(0, 4)
-            cols = columns(k if back else c, p)
-            if p == 0:
+            place_c = q if t == 1 else g % 2 * 2 + g // 2
+            span = q if t == 0 else pl.ds(0, 4)
+            cols = columns(r, p)
+            if t == 0:
                 there = rows.at[span, place_b, place_c, :, cols]
-            elif p == 1:
+            elif t == 1:
                 there = rows.at[place_c, span, place_b, :, cols]
             else:
                 there = rows.at[place_b, place_c, span, :, cols]
@@ -195,13 +201,13 @@
             number = base + g if distant else base + g * 2 + (c if back else k)
             box = box.at[number, span]
             turn = -1 if back else 1
-            to = device(*chip(p, 0, turn * behind, turn * g), k)
+            to = device(*moved(t, 0, turn * behind, turn * g), r if back else k)
             src, dst = (there, box) if back else (box, there)
             arrived = rsem.at[p, int(kind == 0)] if back else xsem.at[q]
             if distant:
                 remote(src, dst, sends.at[p], arrived, to).start()
                 return
-            here = jnp.logical_and(g == 0, k == c)
+            here = jnp.logical_and(g == 0, c == (r if back else k))
 
             @pl.when(here)
             def _():
@@ -214,34 +220,29 @@
         def step(i, carry):
             g = (sign * i + 4) % 4
 
-            def lines(kind, ks):
-                for p in (0, 2):
-                    if p == 0 or KINDS[kind][1] == q:
-                        for k in ks:
-                            message(p, kind, g, k)
+            def batch(kind, pairs):
+                for t in (0, 2):
+                    if t == 0 or KINDS[kind][1] == q:
+                        for r, k in pairs:
+                            message(t, r, kind, g, k)
+                for r, k in pairs:
+                    @pl.when(i == 2 * (r if back else k))
+                    def _():
+                        message(1, r, kind, dx, k)
 
             for kind in kinds:
                 only = KINDS[kind][0] - 1
-                if kind < 3:
-                    lines(kind, (0, 1))
-
-                    @pl.when(i % 2 == 0)
-                    def _():
-                        message(1, kind, dx, i // 2)
+                if back and kind < 3:
+                    batch(kind, ((0, None), (1, None)))
                 elif back:
                     @pl.when(c == only)
                     def _():
-                        lines(kind, (0, 1))
-
-                        @pl.when(i % 2 == 0)
+                        batch(kind, ((0, None), (1, None)))
+                else:
+                    for r in range(2):
+                        @pl.when(c == r)
                         def _():
-                            message(1, kind, dx, i // 2)
-                else:
-                    lines(kind, (only,))
-
-                    @pl.when(i == 0)
-                    def _():
-                        message(1, kind, dx, only)
+                            batch(kind, ((r, 0), (r, 1)) if kind < 3 else ((r, only),))
             return carry
 
         lax.fori_loop(0, 4, step, 0)
@@ -284,7 +285,7 @@
             return carry
 
         lax.fori_loop(0, D // 512, down, 0)
-        exchange(q, True, (1, 2, 3, 4) if q >= NOW else (0, 1, 2, 3, 4))
+        exchange(q, True, (1, 2, 3, 4, 0))
     for q in range(NOW, 4):
         exchange(q, True, (0,))
 
@@ -299,7 +300,7 @@
         await_bytes(ret[p].at[pl.ds(8, 24)], rsem.at[p, 0])
         for b in (1, 2):
             def step(a, carry):
-                near = weigh(line[p, b, a], ret[p][8 * b : 8 * b + 8, a].reshape(128, W[p]))
+                near = jnp.dot(line[p, b, a], ret[p][8 * b : 8 * b + 8, a].reshape(128, W[p]), preferred_element_type=F32)
                 away = weigh(far[p, b - 1, a], ret[p][20 + 4 * b : 24 + 4 * b, a].reshape(64, W[p]))
                 tk[p][b, a] = (near + away).astype(BF16)
                 return carry
@@ -317,7 +318,7 @@
             copy.wait_recv()
         for d in (2, 1, 3, 0):
             a = PLACE[d]
-            total = weigh(line[p, 0, a], ret[p][0:8, a].reshape(128, W[p]))
+            total = jnp.dot(line[p, 0, a], ret[p][0:8, a].reshape(128, W[p]), preferred_element_type=F32)
             total = total + (rb[p][0, a].astype(F32) + rb[p][1, a].astype(F32))
             if d == 0:
                 tot[:, OFF[p] : OFF[p] + W[p]] = total

time: 143 us -> 143 us (level)
  no operation moved by 1% of the time
where the time goes in v3:
time: 143 us
  Pallas kernels  141 us (99%)
  local copies, waits for them, and re-layouts  1.82 us (1%)
    pallas_call x1, Pallas kernels, shards(): pl.pallas_call(kernel, out_shape=jax.ShapeDtypeStruct(tokens.shape, BF16)...  141 us

profile of v3, /device:TPU:1, one launch (start us, length us, event | category | flops | bytes accessed | tf_op | source)
XLA Modules:
  0.0 143.1 jit_solution(18385623199491994949)
XLA Ops:
  0.0 141.2 %shard_map.82 = bf16[64,3584]{1,0:T(8,128)(2,1)} custom-call(bf16[64,3584]{1,0:T(8,128)(2,1)} %tok_ref.1, f32[3584]{0:T(1024)} %gain_ref.1, bf16[1,3584,1024]{2,1,0:T(8,128)(2,1)} %wg_hbm.1, bf16[1,3584,1024]{2,1,0:T(8,128)(2,1)} %wu_hbm.1, bf16[1,1024,3584]{2,1,0:T(8,128)(2,1)} %wd_hbm.1, s32[8,64]{1,0:T(8,128)} %bitcast.3, f32[8,64]{1,0:T(8,128)} %bitcast.4, ...), custom_call_target="tpu_custom_call" | custom-call | flops 23000000512 | bytes 23000000 | tf_op jit(solution)/shard_map/pallas_call | solution.py:358
  141.3 1.8 %copy.10 = bf16[64,3584]{1,0:T(8,128)(2,1)} copy(bf16[64,3584]{1,0:T(8,128)(2,1)} %shard_map.82) | data formatting | bytes 917504
